TPU v7x, 256 devices: a whole 4x4x8 slice. The times are simulated.
256 devices in a mesh: fem: 16 (over z_hi, y), row: 4 (over x), col: 4 (over z_lo, core).
Axes of the slice: x: 4, y: 4, z: 8 (z_hi: 4, z_lo: 2; z = z_hi * 2 + z_lo), core: 2. Of those that a mesh axis runs over, the one named last changes fastest.
Arguments:
- inverse_factor: bfloat16 [256, 1536, 1536], P(('fem', 'row', 'col')), may hold values from -1 to 1.5, as said below
- coupling: bfloat16 [256, 1536, 1024], P(('fem', 'row', 'col')), may hold values from -0.19921875 to 0.19921875
- boundary_tiles: int32 [256, 8], replicated, may hold values from 0 to 15, as said below
- bem_block: float32 [1, 64, 128, 8192], P(None, ('fem', 'row'), None, 'col'), may hold values from -6 to 48
Outputs:
- boundary_factors: float32 [1, 64, 128, 8192], P(None, ('fem', 'row'), None, 'col')
Inputs may be any that keep to these rules, and one draw needn't show every extreme that they name: `inverse_factor`: lower triangular. `boundary_tiles`: each row holds 8 distinct values.
All inputs are finite; a program needn't handle non-finite values.
Results may differ from a plain program's by a relative error of at most 0.0003.
Values may be sent and summed in bfloat16 or wider, within the bound.
A program may use at most 128 MiB of HBM per device.

v0:
```python
import jax
import jax.numpy as jnp
from jax import lax
from jax.sharding import PartitionSpec as P

PW = 256


def broadcast(value, axis, root):
    mine = lax.axis_index(axis) == root
    return lax.psum(jnp.where(mine, value, jnp.zeros_like(value)), axis)


def highest(left, right):
    return jnp.dot(left, right, precision=lax.Precision.HIGHEST)


def series_inverse(strict):
    extent = strict.shape[0]
    identity = jnp.eye(extent, dtype=jnp.float32)
    result = identity - strict
    power = strict
    reach = 2
    while reach < extent:
        power = highest(power, power)
        result = highest(result, identity + power)
        reach = reach * 2
    return result


def eliminate(square):
    extent = square.shape[0]
    places = jnp.arange(extent)

    def sweep(column, current):
        pivot = current[column, column]
        column_values = lax.dynamic_index_in_dim(current, column, 1, keepdims=False)
        row_values = lax.dynamic_index_in_dim(current, column, 0, keepdims=False)
        below = places > column
        scaled = jnp.where(below, column_values / pivot, 0.0)
        current = jnp.where(below[:, None] & (places == column)[None, :], scaled[:, None], current)
        trailing = below[:, None] & below[None, :]
        current = current - jnp.where(trailing, scaled[:, None] * row_values[None, :], 0.0)
        return current

    return lax.fori_loop(0, extent - 1, sweep, square)


def factor(square):
    extent = square.shape[0]
    if extent <= 16:
        packed = eliminate(square)
        lower_inv = series_inverse(jnp.tril(packed, -1))
        pivots = jnp.diagonal(packed)
        unit_upper = jnp.triu(packed) / pivots[:, None]
        upper_inv = series_inverse(jnp.triu(unit_upper, 1)) / pivots[None, :]
        return (packed, lower_inv, upper_inv)
    halfway = extent // 2
    rest = extent - halfway
    leading, first_lower, first_upper = factor(square[:halfway, :halfway])
    right_part = highest(first_lower, square[:halfway, halfway:])
    below_part = highest(square[halfway:, :halfway], first_upper)
    remainder, second_lower, second_upper = factor(
        square[halfway:, halfway:] - highest(below_part, right_part)
    )
    packed = jnp.concatenate(
        [
            jnp.concatenate([leading, right_part], axis=1),
            jnp.concatenate([below_part, remainder], axis=1),
        ],
        axis=0,
    )
    lower_corner = -highest(second_lower, highest(below_part, first_lower))
    upper_corner = -highest(first_upper, highest(right_part, second_upper))
    zeros_right = jnp.zeros((halfway, rest), jnp.float32)
    zeros_below = jnp.zeros((rest, halfway), jnp.float32)
    lower_inv = jnp.concatenate(
        [
            jnp.concatenate([first_lower, zeros_right], axis=1),
            jnp.concatenate([lower_corner, second_lower], axis=1),
        ],
        axis=0,
    )
    upper_inv = jnp.concatenate(
        [
            jnp.concatenate([first_upper, upper_corner], axis=1),
            jnp.concatenate([zeros_below, second_upper], axis=1),
        ],
        axis=0,
    )
    return (packed, lower_inv, upper_inv)


def local(inverse_factor, coupling, boundary_tiles, bem_block):
    fem_count = lax.axis_size("fem")
    row_count = lax.axis_size("row")
    col_count = lax.axis_size("col")
    fem_index = lax.axis_index("fem")
    row_index = lax.axis_index("row")
    col_index = lax.axis_index("col")
    row_tiles = bem_block.shape[0]
    tile_size = bem_block.shape[2]
    local_width = bem_block.shape[3]
    slot_count = boundary_tiles.shape[1]
    class_tiles = row_tiles * fem_count
    per_block = class_tiles // col_count
    coupled = jnp.dot(inverse_factor[0], coupling[0], preferred_element_type=jnp.float32).astype(
        jnp.bfloat16
    )
    schur = lax.dot_general(
        coupled, coupled, (((0,), (0,)), ((), ())), preferred_element_type=jnp.float32
    ).astype(jnp.bfloat16)
    subdomain = (fem_index * row_count + row_index) * col_count + col_index
    chosen = lax.dynamic_index_in_dim(boundary_tiles, subdomain, 0, keepdims=False)
    one_hot = (chosen[None, :] == jnp.arange(class_tiles, dtype=jnp.int32)[:, None]).astype(
        jnp.bfloat16
    )
    row_pick = one_hot.reshape(row_tiles, fem_count, slot_count)
    col_pick = one_hot.reshape(col_count, per_block, slot_count)
    blocks = schur.reshape(slot_count, tile_size, slot_count, tile_size)
    by_rows = jnp.einsum("kga,aibj->gkibj", row_pick, blocks, preferred_element_type=jnp.bfloat16)
    placed = jnp.einsum("cmb,gkibj->gckimj", col_pick, by_rows, preferred_element_type=jnp.bfloat16)
    block_width = per_block * tile_size
    placed = placed.reshape(fem_count * col_count, row_tiles, tile_size, block_width)
    received = lax.all_to_all(placed, ("fem", "col"), split_axis=0, concat_axis=0, tiled=True)
    summed = jnp.sum(received, axis=0, dtype=jnp.float32)
    residue_mask = (jnp.arange(row_count) == row_index).astype(jnp.float32)
    spread = (
        summed.reshape(row_tiles, tile_size, per_block, 1, tile_size)
        * residue_mask[None, None, None, :, None]
    )
    matrix = bem_block[:, 0] + spread.reshape(row_tiles, tile_size, local_width)
    device = fem_index * row_count + row_index
    class_count = fem_count * row_count
    global_rows = (
        (jnp.arange(row_tiles)[:, None] * class_count + device) * tile_size
        + jnp.arange(tile_size)[None, :]
    ).reshape(-1)
    global_cols = col_index * local_width + jnp.arange(local_width)
    panel_tiles = PW // tile_size
    stop_col = PW
    pieces = [
        broadcast(matrix[0], ("fem", "row"), 0 * panel_tiles + member)
        for member in range(panel_tiles)
    ]
    panel_top = jnp.concatenate(pieces, axis=0)
    flattened = matrix.reshape(row_tiles * tile_size, local_width)
    diagonal = jnp.where(col_index == 0, panel_top[:, 0:stop_col], jnp.eye(PW, dtype=jnp.float32))
    packed, lower_inv, upper_inv = factor(diagonal)
    panel_cols = jnp.where(col_index == 0, flattened[:, 0:stop_col], 0.0)
    lower_rows = highest(panel_cols, upper_inv)
    packed, lower_inv, lower_rows = (
        broadcast(packed, "col", 0),
        broadcast(lower_inv, "col", 0),
        broadcast(lower_rows, "col", 0),
    )
    upper_rows = highest(lower_inv, panel_top)
    update = highest(lower_rows, upper_rows)
    below_mask = global_rows >= stop_col
    right_mask = global_cols >= stop_col
    rows_inside = (global_rows >= 0) & (global_rows < stop_col)
    cols_inside = (global_cols >= 0) & (global_cols < stop_col)
    lower_full = jnp.zeros(flattened.shape, jnp.float32).at[:, 0:stop_col].set(lower_rows)
    upper_full = jnp.where(col_index == 0, upper_rows.at[:, 0:stop_col].set(packed), upper_rows)
    gathered = upper_full[jnp.clip(global_rows - 0, 0, PW - 1)]
    result = jnp.where(below_mask[:, None] & right_mask[None, :], flattened - update, flattened)
    result = jnp.where(below_mask[:, None] & cols_inside[None, :], lower_full, result)
    result = jnp.where(rows_inside[:, None] & (global_cols >= 0)[None, :], gathered, result)
    matrix = result.reshape(row_tiles, tile_size, local_width)
    return matrix[:, None]


def solution(mesh):
    placed = (
        P(("fem", "row", "col"), None, None),
        P(("fem", "row", "col"), None, None),
        P(),
        P(None, ("fem", "row"), None, "col"),
    )
    return jax.shard_map(
        local,
        mesh=mesh,
        in_specs=placed,
        out_specs=P(None, ("fem", "row"), None, "col"),
        check_vma=False,
    )
```

profile of v0, /device:TPU:1, one launch (start us, length us, event | category | flops | bytes accessed | tf_op | source)
XLA Modules:
  0.0 1588.3 jit_solution(11219037571044025827)
XLA Ops:
  8.4 18.4 %convert_bitcast_fusion = bf16[128,8,8,128]{3,1,2,0:T(8,128)(2,1)} fusion(bf16[1,1536,1536]{2,1,0:T(8,128)(2,1)} %param.40, bf16[1,1536,1024]{2,1,0:T(8,128)(2,1)S(1)} %copy-done), kind=kOutput, calls=%fused_computation.159 | convolution fusion | flops 8055685120 | bytes 9961472 | tf_op jit(solution)/shard_map/dot_general | solution.py:110
  30.6 5.7 convolution_bitcast_fusion.1
  36.2 9.2 convolution_bitcast_fusion
  45.4 14.5 copy.144
  59.9 13.3 all-to-all-start
  73.3 182.4 %all-to-all-done = bf16[64,1,128,512]{2,3,1,0:T(8,128)(2,1)} async-done(((bf16[64,1,128,512]{2,3,1,0:T(8,128)(2,1)}), bf16[64,1,128,512]{2,3,1,0:T(8,128)(2,1)}, u32[]{:S(2)}, u32[]{:S(2)}) %all-to-all-start) | async-done | bytes 8388640 | tf_op jit(solution)/shard_map/all_to_all | solution.py:125
  271.1 691.8 %all-reduce.36.cloned.1.call-done = (f32[128,2048]{1,0:T(8,128)}, f32[128,2048]{1,0:T(8,128)}) async-done(((f32[128,2048]{1,0:T(8,128)}, f32[128,2048]{1,0:T(8,128)}), (f32[128,2048]{1,0:T(8,128)}, f32[128,2048]{1,0:T(8,128)})) %all-reduce.36.cloned.1.call-update) | async-done | bytes 2097168 | tf_op jit(solution)/shard_map/psum | solution.py:11
  965.9 22.8 %while.242 = (s32[]{:T(128)}, f32[16,16]{0,1:T(8,128)S(1)}, s32[]{:T(128)}) while((s32[]{:T(128)}, f32[16,16]{0,1:T(8,128)S(1)}, s32[]{:T(128)}) %tuple.576), condition=%wide.region_4.5_spmd.clone.clone, body=%wide.region_3.4_spmd.clone.clone.sunk | while | flops 1618 | bytes 4097 | solution.py:46
  992.1 22.9 %while.243 = (s32[]{:T(128)}, f32[16,16]{0,1:T(8,128)S(1)}, s32[]{:T(128)}) while((s32[]{:T(128)}, f32[16,16]{0,1:T(8,128)S(1)}, s32[]{:T(128)}) %tuple.579), condition=%wide.region_6.7_spmd.clone.clone, body=%wide.region_5.6_spmd.clone.clone.sunk | while | flops 1618 | bytes 4097 | solution.py:46
  1018.9 22.8 %while.244 = (s32[]{:T(128)}, f32[16,16]{0,1:T(8,128)S(1)}, s32[]{:T(128)}) while((s32[]{:T(128)}, f32[16,16]{0,1:T(8,128)S(1)}, s32[]{:T(128)}) %tuple.582), condition=%wide.region_8.9_spmd.clone.clone, body=%wide.region_7.8_spmd.clone.clone.sunk | while | flops 1618 | bytes 4097 | solution.py:46
  1045.0 22.9 %while.245 = (s32[]{:T(128)}, f32[16,16]{0,1:T(8,128)S(1)}, s32[]{:T(128)}) while((s32[]{:T(128)}, f32[16,16]{0,1:T(8,128)S(1)}, s32[]{:T(128)}) %tuple.585), condition=%wide.region_10.11_spmd.clone.clone, body=%wide.region_9.10_spmd.clone.clone.sunk | while | flops 1618 | bytes 4097 | solution.py:46
  1076.5 24.4 %while.246 = (s32[]{:T(128)}, f32[16,16]{0,1:T(8,128)S(1)}, s32[]{:T(128)}) while((s32[]{:T(128)}, f32[16,16]{0,1:T(8,128)S(1)}, s32[]{:T(128)}) %tuple.588), condition=%wide.region_12.13_spmd.clone.clone, body=%wide.region_11.12_spmd.clone.clone.sunk | while | flops 1618 | bytes 4097 | solution.py:46
  1110.2 23.0 %while.247 = (s32[]{:T(128)}, f32[16,16]{0,1:T(8,128)S(1)}, s32[]{:T(128)}) while((s32[]{:T(128)}, f32[16,16]{0,1:T(8,128)S(1)}, s32[]{:T(128)}) %tuple.591), condition=%wide.region_14.15_spmd.clone.clone, body=%wide.region_13.14_spmd.clone.clone.sunk | while | flops 1618 | bytes 4097 | solution.py:46
  1146.9 20.9 %while.248 = (s32[]{:T(128)}, f32[16,16]{0,1:T(8,128)S(1)}, s32[]{:T(128)}) while((s32[]{:T(128)}, f32[16,16]{0,1:T(8,128)S(1)}, s32[]{:T(128)}) %tuple.594), condition=%wide.region_16.17_spmd.clone.clone, body=%wide.region_15.16_spmd.clone.clone.sunk | while | flops 1618 | bytes 4097 | solution.py:46
  1176.7 24.4 %while.249 = (s32[]{:T(128)}, f32[16,16]{0,1:T(8,128)S(1)}, s32[]{:T(128)}) while((s32[]{:T(128)}, f32[16,16]{0,1:T(8,128)S(1)}, s32[]{:T(128)}) %tuple.597), condition=%wide.region_18.19_spmd.clone.clone, body=%wide.region_17.18_spmd.clone.clone.sunk | while | flops 1618 | bytes 4097 | solution.py:46
  1221.1 23.4 %while.250 = (s32[]{:T(128)}, f32[16,16]{0,1:T(8,128)S(1)}, s32[]{:T(128)}) while((s32[]{:T(128)}, f32[16,16]{0,1:T(8,128)S(1)}, s32[]{:T(128)}) %tuple.600), condition=%wide.region_20.21_spmd.clone.clone, body=%wide.region_19.20_spmd.clone.clone.sunk | while | flops 1618 | bytes 4097 | solution.py:46
  1252.7 20.9 %while.251 = (s32[]{:T(128)}, f32[16,16]{0,1:T(8,128)S(1)}, s32[]{:T(128)}) while((s32[]{:T(128)}, f32[16,16]{0,1:T(8,128)S(1)}, s32[]{:T(128)}) %tuple.603), condition=%wide.region_22.23_spmd.clone.clone, body=%wide.region_21.22_spmd.clone.clone.sunk | while | flops 1618 | bytes 4097 | solution.py:46
  1279.1 22.8 %while.252 = (s32[]{:T(128)}, f32[16,16]{0,1:T(8,128)S(1)}, s32[]{:T(128)}) while((s32[]{:T(128)}, f32[16,16]{0,1:T(8,128)S(1)}, s32[]{:T(128)}) %tuple.606), condition=%wide.region_24.25_spmd.clone.clone, body=%wide.region_23.24_spmd.clone.clone.sunk | while | flops 1618 | bytes 4097 | solution.py:46
  1305.3 22.9 %while.253 = (s32[]{:T(128)}, f32[16,16]{0,1:T(8,128)S(1)}, s32[]{:T(128)}) while((s32[]{:T(128)}, f32[16,16]{0,1:T(8,128)S(1)}, s32[]{:T(128)}) %tuple.609), condition=%wide.region_26.27_spmd.clone.clone, body=%wide.region_25.26_spmd.clone.clone.sunk | while | flops 1618 | bytes 4097 | solution.py:46
  1334.8 22.8 %while.254 = (s32[]{:T(128)}, f32[16,16]{0,1:T(8,128)S(1)}, s32[]{:T(128)}) while((s32[]{:T(128)}, f32[16,16]{0,1:T(8,128)S(1)}, s32[]{:T(128)}) %tuple.612), condition=%wide.region_28.29_spmd.clone.clone, body=%wide.region_27.28_spmd.clone.clone.sunk | while | flops 1618 | bytes 4097 | solution.py:46
  1361.5 22.1 %while.255 = (s32[]{:T(128)}, f32[16,16]{0,1:T(8,128)S(1)}, s32[]{:T(128)}) while((s32[]{:T(128)}, f32[16,16]{0,1:T(8,128)S(1)}, s32[]{:T(128)}) %tuple.615), condition=%wide.region_30.31_spmd.clone.clone, body=%wide.region_29.30_spmd.clone.clone.sunk | while | flops 1618 | bytes 4097 | solution.py:46
  1394.8 23.4 %while.256 = (s32[]{:T(128)}, f32[16,16]{0,1:T(8,128)S(1)}, s32[]{:T(128)}) while((s32[]{:T(128)}, f32[16,16]{0,1:T(8,128)S(1)}, s32[]{:T(128)}) %tuple.618), condition=%wide.region_32.33_spmd.clone.clone, body=%wide.region_31.32_spmd.clone.clone.sunk | while | flops 1618 | bytes 4097 | solution.py:46
  1427.7 22.8 %while.257 = (s32[]{:T(128)}, f32[16,16]{0,1:T(8,128)S(1)}, s32[]{:T(128)}) while((s32[]{:T(128)}, f32[16,16]{0,1:T(8,128)S(1)}, s32[]{:T(128)}) %tuple.621), condition=%wide.region_34.35_spmd.clone.clone, body=%wide.region_33.34_spmd.clone.clone.sunk | while | flops 1618 | bytes 4097 | solution.py:46
  1477.7 86.1 %all-reduce.38.cloned.1.call-done = (f32[256,256]{1,0:T(8,128)}, f32[256,256]{1,0:T(8,128)}, f32[128,256]{1,0:T(8,128)}) async-done(((f32[256,256]{1,0:T(8,128)}, f32[256,256]{1,0:T(8,128)}, f32[128,256]{1,0:T(8,128)}), (f32[256,256]{1,0:T(8,128)}, f32[256,256]{1,0:T(8,128)}, f32[128,256]{1,0:T(8,128)})) %all-reduce.38.cloned.1.call-update) | async-done | bytes 655376 | tf_op jit(solution)/shard_map/psum | solution.py:11
  (1860 shorter events, 548.4 us)
Async XLA Ops:
  59.9 195.8 %all-to-all-start = ((bf16[64,1,128,512]{2,3,1,0:T(8,128)(2,1)}), bf16[64,1,128,512]{2,3,1,0:T(8,128)(2,1)}, u32[]{:S(2)}, u32[]{:S(2)}) async-start(bf16[64,1,128,512]{2,3,1,0:T(8,128)(2,1)} %bitcast.650), calls=%async_computation | async-start | bytes 16777216 | tf_op jit(solution)/shard_map/all_to_all | solution.py:125
  73.3 889.6 %all-reduce.36.cloned.1.call-start = ((), (), s32[]{:S(2)}) async-start(), calls=%async_computation.1 | async-start | bytes 4194304 | tf_op jit(solution)/shard_map/psum | solution.py:11
  270.8 1293.0 %all-reduce.38.cloned.1.call-start = ((), (), s32[]{:S(2)}) async-start(), calls=%async_computation.2 | async-start | bytes 1310720 | tf_op jit(solution)/shard_map/psum | solution.py:11
  271.1 772.2 %copy-start.119 = (s32[16]{0:T(128)}, s32[16]{0:T(128)S(1)}, u32[]{:S(2)}) copy-start(s32[16]{0:T(128)S(1)} %iota_add_fusion.1) | copy-start | bytes 196
  991.0 84.1 %copy-start.14 = (f32[16,16]{1,0:T(8,128)}, f32[16,16]{1,0:T(8,128)S(1)}, u32[]{:S(2)}) copy-start(f32[16,16]{1,0:T(8,128)S(1)} %convolution_divide_fusion.15) | copy-start | bytes 3076
  1017.7 53.7 %copy-start.28 = (f32[32,32]{1,0:T(8,128)}, f32[32,32]{1,0:T(8,128)S(1)}, u32[]{:S(2)}) copy-start(f32[32,32]{1,0:T(8,128)S(1)} %fusion.141) | copy-start | bytes 12292
  1018.4 58.1 %copy-start.20 = (f32[16,16]{1,0:T(8,128)}, f32[16,16]{1,0:T(8,128)S(1)}, u32[]{:S(2)}) copy-start(f32[16,16]{1,0:T(8,128)S(1)} %convolution_negate_fusion.28) | copy-start | bytes 3076
  1018.5 56.9 %copy-start.22 = (f32[16,32]{1,0:T(8,128)}, f32[16,32]{1,0:T(8,128)S(1)}, u32[]{:S(2)}) copy-start(f32[16,32]{1,0:T(8,128)S(1)} %concatenate.438) | copy-start | bytes 6148
  1018.7 56.1 %copy-start.30 = (f32[32,32]{1,0:T(8,128)}, f32[32,32]{1,0:T(8,128)S(1)}, u32[]{:S(2)}) copy-start(f32[32,32]{1,0:T(8,128)S(1)} %fusion.143) | copy-start | bytes 12292
  1071.6 73.7 %copy-start.16 = (f32[32,64]{1,0:T(8,128)}, f32[32,64]{1,0:T(8,128)S(1)}, u32[]{:S(2)}) copy-start(f32[32,64]{1,0:T(8,128)S(1)} %concatenate.450) | copy-start | bytes 24580
  1075.2 136.6 %copy-start.10 = (f32[64,64]{1,0:T(8,128)}, f32[64,64]{1,0:T(8,128)S(1)}, u32[]{:S(2)}) copy-start(f32[64,64]{1,0:T(8,128)S(1)} %fusion.107) | copy-start | bytes 49156
  1107.5 102.5 %copy-start.53 = (f32[16,16]{1,0:T(8,128)}, f32[16,16]{1,0:T(8,128)S(1)}, u32[]{:S(2)}) copy-start(f32[16,16]{1,0:T(8,128)S(1)} %convolution_divide_fusion.11) | copy-start | bytes 3076
  1146.8 63.1 %copy-start.33 = (f32[32,32]{1,0:T(8,128)S(1)}, f32[32,32]{1,0:T(8,128)}, u32[]{:S(2)}) copy-start(f32[32,32]{1,0:T(8,128)} %copy-done.32) | copy-start | bytes 12292
  1210.1 66.3 %copy-start.120 = (s32[16]{0:T(128)S(1)}, s32[16]{0:T(128)}, u32[]{:S(2)}) copy-start(s32[16]{0:T(128)} %copy-done.119) | copy-start | bytes 196
  1221.1 57.2 %copy-start.8 = (f32[128,128]{1,0:T(8,128)S(1)}, f32[128,128]{1,0:T(8,128)}, u32[]{:S(2)}) copy-start(f32[128,128]{1,0:T(8,128)} %copy-done.7) | copy-start | bytes 196612
  1277.5 56.2 %copy-start.24 = (f32[16,32]{1,0:T(8,128)}, f32[16,32]{1,0:T(8,128)S(1)}, u32[]{:S(2)}) copy-start(f32[16,32]{1,0:T(8,128)S(1)} %concatenate.481) | copy-start | bytes 6148
  1278.3 55.4 %copy-start.25 = (f32[16,16]{1,0:T(8,128)}, f32[16,16]{1,0:T(8,128)S(1)}, u32[]{:S(2)}) copy-start(f32[16,16]{1,0:T(8,128)S(1)} %convolution_negate_fusion.20) | copy-start | bytes 3076
  1278.5 54.6 %copy-start.37 = (f32[32,32]{1,0:T(8,128)}, f32[32,32]{1,0:T(8,128)S(1)}, u32[]{:S(2)}) copy-start(f32[32,32]{1,0:T(8,128)S(1)} %fusion.133) | copy-start | bytes 12292
  1278.7 54.4 %copy-start.39 = (f32[32,32]{1,0:T(8,128)}, f32[32,32]{1,0:T(8,128)S(1)}, u32[]{:S(2)}) copy-start(f32[32,32]{1,0:T(8,128)S(1)} %fusion.135) | copy-start | bytes 12292
  1304.6 80.7 %copy-start.76 = (f32[16,16]{1,0:T(8,128)}, f32[16,16]{1,0:T(8,128)S(1)}, u32[]{:S(2)}) copy-start(f32[16,16]{1,0:T(8,128)S(1)} %fusion.239) | copy-start | bytes 3076
  1331.6 60.6 %copy-start.46 = (f32[32,64]{1,0:T(8,128)}, f32[32,64]{1,0:T(8,128)S(1)}, u32[]{:S(2)}) copy-start(f32[32,64]{1,0:T(8,128)S(1)} %concatenate.493) | copy-start | bytes 24580
  1360.2 58.0 %copy-start.52 = (f32[16,16]{1,0:T(8,128)}, f32[16,16]{1,0:T(8,128)S(1)}, u32[]{:S(2)}) copy-start(f32[16,16]{1,0:T(8,128)S(1)} %convolution_divide_fusion.3) | copy-start | bytes 3076
  1384.3 70.2 %copy-start.6 = (f32[128,128]{0,1:T(8,128)S(1)}, f32[128,128]{0,1:T(8,128)}, u32[]{:S(2)}) copy-start(f32[128,128]{0,1:T(8,128)} %copy-done.5) | copy-start | bytes 196612
  1418.2 51.5 %copy-start.15 = (f32[16,16]{1,0:T(8,128)S(1)}, f32[16,16]{1,0:T(8,128)}, u32[]{:S(2)}) copy-start(f32[16,16]{1,0:T(8,128)} %copy-done.14) | copy-start | bytes 3076
  (100 other events, 1542.9 us)
Sparse Core Ops, SparseCore 0:
  270.9 691.9 all-reduce.35
  1477.1 86.6 all-reduce.37
where the time goes:
time: 1600 us; the launch traced here: 1590 us
  waiting for transfers between devices  960 us (60%)
  local copies, waits for them, and re-layouts  250 us (16%)
  other arithmetic  194 us (12%)
  matrix products  152 us (10%)
    psum x2, waiting for transfers between devices, broadcast(): return lax.psum(jnp.where(mine, value, jnp.zeros_like(value)), axis)  778 us
    all_to_all x1, waiting for transfers between devices, local(): lax.all_to_all(placed, ('fem', 'col'), split_axis=0, concat_axis=0, tiled...  182 us
    broadcast_in_dim x240, other arithmetic, sweep(): jnp.where(below[:, None] & (places == column)[None, :], scaled[:, None],...  153 us
    dynamic_slice x240, local copies, waits for them, and re-layouts, sweep(): pivot = current[column, column]  145 us
    dot_general x300, matrix products, highest(): return jnp.dot(left, right, precision=lax.Precision.HIGHEST)  119 us
    dynamic_slice x240, local copies, waits for them, and re-layouts, sweep(): row_values = lax.dynamic_index_in_dim(current, column, 0, keepdims=False)  44.5 us
  transfers between devices with their start and end apart: 3, of which 3 were waited for; matrix products, arithmetic and copies ran while one was open for 0% of the time, Pallas kernels for 0%

commit v1 on v0

v1 whole, which is shorter than its diff:
```python
import jax
import jax.numpy as jnp
from jax import lax
from jax.experimental import pallas as pl
from jax.experimental.pallas import tpu as pltpu
from jax.sharding import PartitionSpec as P

MESH = pl.DeviceIdType.MESH
F32 = jnp.float32
BF16 = jnp.bfloat16
T = 128
VMEM_LIMIT = 60 * 1024 * 1024


def highest(left, right):
    return jnp.dot(left, right, precision=lax.Precision.HIGHEST, preferred_element_type=F32)


def contribution_kernel(place_ref, factor_ref, coupling_ref, out_ref, coupled):
    order, width = coupling_ref.shape
    step = 256
    out_ref[...] = jnp.zeros_like(out_ref)
    for i in range(order // step):
        for n in range(width // 512):
            coupled[i * step : (i + 1) * step, n * 512 : (n + 1) * 512] = jnp.dot(
                factor_ref[i * step : (i + 1) * step, : (i + 1) * step],
                coupling_ref[: (i + 1) * step, n * 512 : (n + 1) * 512],
                preferred_element_type=F32,
            ).astype(BF16)
    for pair in range(width // step):
        for n in range(width // 512):
            block = lax.dot_general(
                coupled[:, pair * step : (pair + 1) * step],
                coupled[:, n * 512 : (n + 1) * 512],
                (((0,), (0,)), ((), ())),
                preferred_element_type=F32,
            ).astype(BF16)
            for half in range(step // T):
                place = place_ref[pair * (step // T) + half]
                for j in range(512 // T):
                    out_ref[place, n * (512 // T) + j] = block[
                        half * T : (half + 1) * T, j * T : (j + 1) * T
                    ]


def contribution(places, factor, coupling, tiles):
    order, width = coupling.shape
    slots = width // T
    return pl.pallas_call(
        contribution_kernel,
        out_shape=jax.ShapeDtypeStruct((tiles, slots, T, T), BF16),
        in_specs=[
            pl.BlockSpec(memory_space=pltpu.SMEM),
            pl.BlockSpec(memory_space=pltpu.VMEM),
            pl.BlockSpec(memory_space=pltpu.VMEM),
        ],
        out_specs=pl.BlockSpec(memory_space=pltpu.VMEM),
        scratch_shapes=[pltpu.VMEM((order, width), BF16)],
        compiler_params=pltpu.CompilerParams(vmem_limit_bytes=VMEM_LIMIT),
        name="contribution",
    )(places, factor, coupling)


def assemble_kernel(
    slot_ref, weight_ref, dense_ref, bem_ref,
    m_ref, panel_ref, diag_ref, cols_ref,
    recv, acc, other, plus0, minus0, plus, minus, xpart, ypart, zpart,
    y_send, y_recv, c_send, c_recv, r_send, r_recv,
    px_send, px_recv, py_send, py_recv, pz_send, pz_recv,
    gy_send, gy_recv, gx_send, gx_recv, d_send, d_recv, a_send, a_recv,
):
    f = lax.axis_index("fem")
    r = lax.axis_index("row")
    c = lax.axis_index("col")
    zh, y = f // 4, f % 4
    zl, core = c // 2, c % 2
    z = zh * 2 + zl

    def at_y(d):
        return (zh * 4 + (y + d) % 4, r, c)

    def at_z(d):
        to = (z + d + 8) % 8
        return ((to // 2) * 4 + y, r, (to % 2) * 2 + core)

    def at_zh(d):
        return (((zh + d) % 4) * 4 + y, r, c)

    def at_x(d):
        return (f, (r + d) % 4, c)

    def at_col(d):
        return (f, r, (c + d) % 4)

    partner = (f, r, c + 1 - 2 * core)

    def copy(src, dst, send, recv_sem, to):
        return pltpu.make_async_remote_copy(
            src_ref=src, dst_ref=dst, send_sem=send, recv_sem=recv_sem,
            device_id=to, device_id_type=MESH,
        )

    barrier = pltpu.get_barrier_semaphore()
    greet = [at_y(d) for d in (1, 2, 3)] + [at_z(1), at_z(-1)]
    greet += [at_zh(d) for d in (1, 2, 3)] + [at_x(d) for d in (1, 2, 3)]
    greet += [at_col(d) for d in (1, 2, 3)]
    for to in greet:
        pl.semaphore_signal(barrier, inc=1, device_id=to, device_id_type=MESH)
    pl.semaphore_wait(barrier, len(greet))

    y_copies = []
    for q in range(4):
        for d in (1, 2, 3):
            one = copy(
                dense_ref.at[q * 4 + (y + d) % 4], recv.at[d - 1, q],
                y_send.at[d - 1, q], y_recv.at[d - 1, q], at_y(d),
            )
            one.start()
            y_copies.append(one)
    for one in y_copies:
        one.wait()

    def gather(step, carry):
        q = step // 4
        b4 = step % 4
        side = (b4 % 2 + core) % 2
        zto = q * 2 + b4 // 2
        for i in range(4):
            b = b4 * 4 + i
            total = dense_ref[q * 4 + y, slot_ref[b]].astype(F32) * weight_ref[b]
            for d in (1, 2, 3):
                total += recv[d - 1, q, slot_ref[d * 16 + b]].astype(F32) * weight_ref[d * 16 + b]
            acc[side, zto, :, i * T : (i + 1) * T] = total
        return carry

    lax.fori_loop(0, 16, gather, 0)

    swap = copy(acc.at[1], other, c_send, c_recv, partner)
    swap.start()
    swap.wait()

    half = T // 2
    far = (z + 4) % 8
    acc[0, far] = acc[0, far] + other[far]
    ring = []

    def hop(src, dst, lane, d):
        one = copy(src, dst, r_send.at[lane, d], r_recv.at[lane, d], at_z(1 - 2 * lane))
        one.start()
        ring.append(one)
        return one

    up = hop(acc.at[0, far, pl.ds(0, half)], plus0, 0, 0)
    down = hop(acc.at[0, far, pl.ds(half, half)], minus0, 1, 0)
    for d in (3, 2, 1):
        zp = (z + d) % 8
        zm = (z + 8 - d) % 8
        acc[0, zp] = acc[0, zp] + other[zp]
        acc[0, zm] = acc[0, zm] + other[zm]
        up.wait_recv()
        if d == 3:
            acc[0, zp, 0:half] = acc[0, zp, 0:half] + plus0[...]
        else:
            acc[0, zp] = acc[0, zp] + plus[2 - d]
        up = hop(acc.at[0, zp], plus.at[3 - d], 0, 4 - d)
        down.wait_recv()
        if d == 3:
            acc[0, zm, half:T] = acc[0, zm, half:T] + minus0[...]
        else:
            acc[0, zm] = acc[0, zm] + minus[2 - d]
        down = hop(acc.at[0, zm], minus.at[3 - d], 1, 4 - d)
    m_ref[...] = bem_ref[...]
    up.wait_recv()
    down.wait_recv()
    for i in range(4):
        lanes = pl.ds(pl.multiple_of((i * 4 + r) * T, T), T)
        part = pl.ds(i * T, T)
        m_ref[:, lanes] = m_ref[:, lanes] + (
            acc[0, z, :, part] + other[z, :, part] + plus[2, :, part] + minus[2, :, part]
        )
    for one in ring:
        one.wait_send()

    def col_copies():
        return [
            copy(m_ref.at[:, pl.ds(0, 256)], cols_ref, a_send.at[d - 1], a_recv, at_col(d))
            for d in (1, 2, 3)
        ]

    @pl.when(c == 0)
    def _():
        for one in col_copies():
            one.start()

    def x_copies():
        return [
            copy(
                m_ref.at[:, pl.ds(pl.multiple_of(((r + d) % 4) * 512, 512), 512)], xpart.at[r % 2],
                px_send.at[d - 1], px_recv.at[r % 2], at_x(d),
            )
            for d in (1, 2, 3)
        ]

    def y_parts():
        return [
            copy(
                xpart.at[:, pl.ds(d * 32, 32)], ypart, py_send.at[d - 1], py_recv, (d, r, c)
            )
            for d in (1, 2, 3)
        ]

    def z_parts():
        return [copy(ypart, ypart, pz_send.at[d - 1], pz_recv, at_zh(d)) for d in (1, 2, 3)]

    @pl.when(f == 0)
    def _():
        @pl.when(r < 2)
        def _():
            for one in x_copies():
                one.start()
            xpart[r % 2] = m_ref[:, pl.ds(pl.multiple_of((r % 2) * 512, 512), 512)]

        for m in range(2):
            @pl.when(r != m)
            def _():
                copy(xpart.at[m], xpart.at[m], px_send.at[0], px_recv.at[m], at_x(1)).wait_recv()

        for one in y_parts():
            one.start()
        ypart[...] = xpart[:, 0:32]

    @pl.when((zh == 0) & (y != 0))
    def _():
        copy(ypart, ypart, py_send.at[0], py_recv, at_x(1)).wait_recv()

    @pl.when(zh == 0)
    def _():
        for one in z_parts():
            one.start()

    @pl.when(zh != 0)
    def _():
        copy(ypart, ypart, pz_send.at[0], pz_recv, at_x(1)).wait_recv()

    rows = pl.ds(pl.multiple_of(y * 32, 32), 32)
    gy = [
        copy(ypart, zpart.at[:, rows], gy_send.at[d - 1], gy_recv.at[d - 1], at_y(d))
        for d in (1, 2, 3)
    ]
    for one in gy:
        one.start()
    zpart[:, rows] = ypart[...]
    for one in gy:
        one.wait_recv()
    gx = [
        copy(zpart, panel_ref.at[r], gx_send.at[d - 1], gx_recv.at[d - 1], at_x(d))
        for d in (1, 2, 3)
    ]
    for one in gx:
        one.start()
    panel_ref[r] = zpart[...]
    for one in gx:
        one.wait_recv()

    def diag_copies():
        return [
            copy(panel_ref.at[0, :, :, pl.ds(0, 256)], diag_ref, d_send.at[d - 1], d_recv, at_col(d))
            for d in (1, 2, 3)
        ]

    @pl.when(c == 0)
    def _():
        for one in diag_copies():
            one.start()
        diag_ref[...] = panel_ref[0, :, :, 0:256]
        cols_ref[...] = m_ref[:, 0:256]
        for one in diag_copies() + col_copies():
            one.wait_send()

    @pl.when(c != 0)
    def _():
        copy(cols_ref, cols_ref, a_send.at[0], a_recv, at_col(1)).wait_recv()
        copy(diag_ref, diag_ref, d_send.at[0], d_recv, at_col(1)).wait_recv()

    @pl.when(f == 0)
    def _():
        @pl.when(r < 2)
        def _():
            for one in x_copies():
                one.wait_send()

        for one in y_parts():
            one.wait_send()

    @pl.when(zh == 0)
    def _():
        for one in z_parts():
            one.wait_send()

    for one in gy + gx:
        one.wait_send()


def assemble(slots, weights, dense, bem):
    vmem = pl.BlockSpec(memory_space=pltpu.VMEM)
    smem = pl.BlockSpec(memory_space=pltpu.SMEM)
    dma = pltpu.SemaphoreType.DMA
    return pl.pallas_call(
        assemble_kernel,
        out_shape=[
            jax.ShapeDtypeStruct((T, 2048), F32),
            jax.ShapeDtypeStruct((4, 2, T, 512), F32),
            jax.ShapeDtypeStruct((2, T, 256), F32),
            jax.ShapeDtypeStruct((T, 256), F32),
        ],
        in_specs=[smem, smem, vmem, vmem],
        out_specs=[vmem, vmem, vmem, vmem],
        scratch_shapes=[
            pltpu.VMEM((3, 4, 8, T, T), BF16),
            pltpu.VMEM((2, 8, T, 512), F32),
            pltpu.VMEM((8, T, 512), F32),
            pltpu.VMEM((T // 2, 512), F32),
            pltpu.VMEM((T // 2, 512), F32),
            pltpu.VMEM((3, T, 512), F32),
            pltpu.VMEM((3, T, 512), F32),
            pltpu.VMEM((2, T, 512), F32),
            pltpu.VMEM((2, 32, 512), F32),
            pltpu.VMEM((2, T, 512), F32),
            dma((3, 4)), dma((3, 4)), dma, dma, dma((2, 4)), dma((2, 4)),
            dma((3,)), dma((2,)), dma((3,)), dma, dma((3,)), dma,
            dma((3,)), dma((3,)), dma((3,)), dma((3,)), dma((3,)), dma, dma((3,)), dma,
        ],
        compiler_params=pltpu.CompilerParams(
            collective_id=0, has_side_effects=True, vmem_limit_bytes=VMEM_LIMIT
        ),
        name="assemble",
    )(slots, weights, dense, bem)


def eliminate(work, unit, first, last):
    lanes = lax.broadcasted_iota(jnp.int32, (1, T), 1)
    for j in range(T):
        top = (j // 8) * 8
        count = last - top
        row = work[j : j + 1, :]
        inverse_pivot = 1.0 / row[:, j : j + 1]
        below = lax.broadcasted_iota(jnp.int32, (count, 1), 0) + top > j
        block = work[top:last, :]
        scaled = jnp.where(below, block[:, j : j + 1] * inverse_pivot, 0.0)
        right = jnp.where(lanes > j, row, 0.0)
        work[top:last, :] = jnp.where(
            (lanes == j) & below, scaled, block - scaled * right
        )
        unit[top:T, :] = unit[top:T, :] - scaled[: T - top] * unit[j : j + 1, :]


def update_kernel(m_ref, panel_ref, diag_ref, cols_ref, out_ref, work, unit):
    f = lax.axis_index("fem")
    r = lax.axis_index("row")
    c = lax.axis_index("col")
    identity = (
        lax.broadcasted_iota(jnp.int32, (T, T), 0) == lax.broadcasted_iota(jnp.int32, (T, T), 1)
    ).astype(F32)
    work[0:T, :] = diag_ref[0, :, 0:T]
    work[T : 2 * T, :] = diag_ref[1, :, 0:T]
    work[2 * T : 3 * T, :] = cols_ref[:, 0:T]
    unit[...] = identity
    eliminate(work, unit, 0, 3 * T)
    first = work[...]
    first_inv = unit[...]
    upper = highest(first_inv, diag_ref[0, :, T:256])
    work[0:T, :] = diag_ref[1, :, T:256] - highest(first[T : 2 * T], upper)
    work[T : 2 * T, :] = cols_ref[:, T:256] - highest(first[2 * T :], upper)
    unit[...] = identity
    eliminate(work, unit, 0, 2 * T)
    second = work[0 : 2 * T, :]
    second_inv = unit[...]
    corner = -highest(second_inv, highest(first[T : 2 * T], first_inv))
    lower = second[T:]
    is_panel = (f == 0) & (r < 2)
    left = jnp.where(
        is_panel,
        jnp.where(r == 0, first_inv, corner),
        -(highest(first[2 * T :], first_inv) + highest(lower, corner)),
    )
    right = jnp.where(
        is_panel,
        jnp.where(r == 0, jnp.zeros_like(second_inv), second_inv),
        -highest(lower, second_inv),
    )
    keep = jnp.where(is_panel, 0.0, 1.0).astype(F32)
    for n in range(4):
        cut = pl.ds(n * 512, 512)
        out_ref[:, cut] = (
            m_ref[:, cut] * keep
            + highest(left, panel_ref[n, 0])
            + highest(right, panel_ref[n, 1])
        )

    @pl.when(c == 0)
    def _():
        out_ref[:, 0:T] = jnp.where(
            is_panel, jnp.where(r == 0, first[0:T], first[T : 2 * T]), first[2 * T :]
        )
        out_ref[:, T:256] = jnp.where(
            is_panel, jnp.where(r == 0, upper, second[0:T]), lower
        )


def update(matrix, panel, diag, cols):
    vmem = pl.BlockSpec(memory_space=pltpu.VMEM)
    return pl.pallas_call(
        update_kernel,
        out_shape=jax.ShapeDtypeStruct(matrix.shape, F32),
        in_specs=[vmem] * 4,
        out_specs=vmem,
        scratch_shapes=[pltpu.VMEM((3 * T, T), F32), pltpu.VMEM((T, T), F32)],
        compiler_params=pltpu.CompilerParams(vmem_limit_bytes=VMEM_LIMIT),
        name="update",
    )(matrix, panel, diag, cols)


def local(inverse_factor, coupling, boundary_tiles, bem_block):
    f = lax.axis_index("fem")
    r = lax.axis_index("row")
    c = lax.axis_index("col")
    rows = lax.axis_size("row")
    columns = lax.axis_size("col")
    tiles = lax.axis_size("fem")
    y = f % 4
    sources = (((f // 4) * 4 + (y - jnp.arange(4)) % 4) * rows + r) * columns + c
    lists = boundary_tiles[sources]
    match = lists[:, :, None] == jnp.arange(tiles, dtype=jnp.int32)[None, None, :]
    slots = jnp.sum(
        jnp.where(match, jnp.arange(lists.shape[1], dtype=jnp.int32)[None, :, None], 0), axis=1
    ).reshape(-1)
    weights = jnp.any(match, axis=1).astype(F32).reshape(-1)
    dense = contribution(lists[0], inverse_factor[0], coupling[0], tiles)
    matrix, panel, diag, cols = assemble(slots, weights, dense, bem_block[0, 0])
    return update(matrix, panel, diag, cols)[None, None]


def solution(mesh):
    placed = (
        P(("fem", "row", "col"), None, None),
        P(("fem", "row", "col"), None, None),
        P(),
        P(None, ("fem", "row"), None, "col"),
    )
    return jax.shard_map(
        local,
        mesh=mesh,
        in_specs=placed,
        out_specs=P(None, ("fem", "row"), None, "col"),
        check_vma=False,
    )
```

time: 1600 us -> 201 us (0.13)
  the two profiles are of different devices: /device:TPU:1 before, /device:TPU:229 now
where the time goes in v1:
time: 201 us
  Pallas kernels  197 us (98%)
  local copies, waits for them, and re-layouts  3.17 us (2%)
    pallas_call x1, Pallas kernels, assemble(): pl.pallas_call(assemble_kernel, out_shape=[jax.ShapeDtypeStruct((T, 2048)...  156 us
    pallas_call x1, Pallas kernels, update(): pl.pallas_call(update_kernel, out_shape=jax.ShapeDtypeStruct(matrix.shape...  29.3 us
    pallas_call x1, Pallas kernels, contribution(): pl.pallas_call(contribution_kernel, out_shape=jax.ShapeDtypeStruct((tiles...  12.1 us

profile of v1, /device:TPU:229, one launch (start us, length us, event | category | flops | bytes accessed | tf_op | source)
XLA Modules:
  0.0 200.7 jit_solution(18055537571878389125)
XLA Ops:
  0.0 0.8 copy.6
  0.9 0.6 gather_fusion
  1.4 0.1 fusion
  1.5 0.5 slice_bitcast_fusion.place_ref
  2.0 0.1 select_reduce_fusion
  2.1 0.6 reshape.72.slot_ref
  2.7 0.7 reshape.73.weight_ref
  3.4 12.1 %contribution.1.dense_ref = bf16[16,8,128,128]{3,2,1,0:T(8,128)(2,1)} custom-call(s32[8]{0:T(128)} %slice_bitcast_fusion.place_ref, bf16[1536,1536]{1,0:T(8,128)(2,1)} %bitcast.8, bf16[1536,1024]{1,0:T(8,128)(2,1)} %bitcast.9), custom_call_target="tpu_custom_call" | custom-call | tf_op jit(solution)/shard_map/contribution/pallas_call | solution.py:49
  15.5 155.9 %assemble.1 = (f32[128,2048]{1,0:T(8,128)}, f32[4,2,128,512]{3,2,1,0:T(8,128)}, f32[2,128,256]{2,1,0:T(8,128)}, f32[128,256]{1,0:T(8,128)}) custom-call(s32[64]{0:T(128)} %reshape.72.slot_ref, f32[64]{0:T(128)} %reshape.73.weight_ref, bf16[16,8,128,128]{3,2,1,0:T(8,128)(2,1)} %contribution.1.dense_ref, f32[128,2048]{1,0:T(8,128)} %bitcast.10), custom_call_target="tpu_custom_call" | custom-call | tf_op jit(solution)/shard_map/assemble/pallas_call | solution.py:308
  171.4 29.3 %update.1 = f32[128,2048]{1,0:T(8,128)} custom-call(f32[128,2048]{1,0:T(8,128)} %get-tuple-element.9.m_ref, f32[4,2,128,512]{3,2,1,0:T(8,128)} %get-tuple-element.10.panel_ref, f32[2,128,256]{2,1,0:T(8,128)} %get-tuple-element.11.diag_ref, f32[128,256]{1,0:T(8,128)} %get-tuple-element.12.cols_ref), custom_call_target="tpu_custom_call" | custom-call | tf_op jit(solution)/shard_map/update/pallas_call | solution.py:412
  (3 shorter events, 0.0 us)

commit v2 on v0

v2 whole, which is shorter than its diff:
```python
import jax
import jax.numpy as jnp
from jax import lax
from jax.experimental import pallas as pl
from jax.experimental.pallas import tpu as pltpu
from jax.sharding import PartitionSpec as P

MESH = pl.DeviceIdType.MESH
F32 = jnp.float32
BF16 = jnp.bfloat16
T = 128
VMEM_LIMIT = 60 * 1024 * 1024


def highest(left, right):
    return jnp.dot(left, right, precision=lax.Precision.HIGHEST, preferred_element_type=F32)


def contribution_kernel(
    tiles_ref, factor_ref, coupling_ref, out_ref, slot_ref, weight_ref, coupled
):
    f = lax.axis_index("fem")
    r = lax.axis_index("row")
    c = lax.axis_index("col")
    order, width = coupling_ref.shape
    tiles, slots = out_ref.shape[0], out_ref.shape[1]
    step = 256
    for i in range(4 * tiles):
        slot_ref[i] = 0
        weight_ref[i] = 0.0
    for d in range(4):
        source = (((f // 4) * 4 + (f + 4 - d) % 4) * 4 + r) * 4 + c
        for k in range(slots):
            tile = tiles_ref[source, k]
            slot_ref[d * tiles + tile] = k
            weight_ref[d * tiles + tile] = 1.0
    me = (f * 4 + r) * 4 + c
    out_ref[...] = jnp.zeros_like(out_ref)
    for i in range(order // step):
        for n in range(width // 512):
            coupled[i * step : (i + 1) * step, n * 512 : (n + 1) * 512] = jnp.dot(
                factor_ref[i * step : (i + 1) * step, : (i + 1) * step],
                coupling_ref[: (i + 1) * step, n * 512 : (n + 1) * 512],
                preferred_element_type=F32,
            ).astype(BF16)
    for pair in range(width // step):
        for n in range(width // 512):
            block = lax.dot_general(
                coupled[:, pair * step : (pair + 1) * step],
                coupled[:, n * 512 : (n + 1) * 512],
                (((0,), (0,)), ((), ())),
                preferred_element_type=F32,
            ).astype(BF16)
            for half in range(step // T):
                place = tiles_ref[me, pair * (step // T) + half]
                for j in range(512 // T):
                    out_ref[place, n * (512 // T) + j] = block[
                        half * T : (half + 1) * T, j * T : (j + 1) * T
                    ]


def contribution(boundary_tiles, factor, coupling, tiles):
    order, width = coupling.shape
    slots = width // T
    smem = pl.BlockSpec(memory_space=pltpu.SMEM)
    vmem = pl.BlockSpec(memory_space=pltpu.VMEM)
    return pl.pallas_call(
        contribution_kernel,
        out_shape=[
            jax.ShapeDtypeStruct((tiles, slots, T, T), BF16),
            jax.ShapeDtypeStruct((4 * tiles,), jnp.int32),
            jax.ShapeDtypeStruct((4 * tiles,), F32),
        ],
        in_specs=[smem, vmem, vmem],
        out_specs=[vmem, smem, smem],
        scratch_shapes=[pltpu.VMEM((order, width), BF16)],
        compiler_params=pltpu.CompilerParams(vmem_limit_bytes=VMEM_LIMIT),
        name="contribution",
    )(boundary_tiles, factor, coupling)


def eliminate_part(work, unit, part, last):
    lanes = lax.broadcasted_iota(jnp.int32, (1, T), 1)
    top = part * 32
    count = last - top
    place = lax.broadcasted_iota(jnp.int32, (count, 1), 0) + top

    def block(step, carry):
        start = pl.multiple_of(top + step * 8, 8)
        for t in range(8):
            row = work[pl.ds(start + t, 1), :]
            unit_row = unit[pl.ds(start + t, 1), :]
            inverse_pivot = 1.0 / row[:, t : t + 1]
            below = place > start + t
            body = work[top:last, :]
            scaled = jnp.where(below, body[:, t : t + 1] * inverse_pivot, 0.0)
            right = jnp.where((lanes > t) & (lanes < T - start), row, 0.0)
            work[top:last, :] = jnp.where((lanes == t) & below, scaled, body - scaled * right)
            unit[top:T, :] = unit[top:T, :] - scaled[: T - top] * unit_row
        work[top:last, :] = pltpu.roll(work[top:last, :], T - 8, 1)
        return carry

    lax.fori_loop(0, 4, block, 0)


def turn_back(work):
    for part in range(3):
        cut = slice(part * 32, (part + 1) * 32)
        work[cut, :] = pltpu.roll(work[cut, :], (part + 1) * 32, 1)


def solve_kernel(
    slot_ref, weight_ref, dense_ref, bem_ref,
    out_ref,
    recv0, recv1, recv2, recv3, acc, other, plus0, minus0, plus, minus,
    xpart, ypart, zpart, panel,
    prow, psum, pother, pz, piece, pa32, pa, atile,
    dy32, d8, gq, g32, diag, cols,
    work, unit,
    y_send, y_recv, c_send, c_recv, r_send, r_recv,
    px_send, px_recv, py_send, py_recv, pz_send, pz_recv, gy_send, gy_recv, gx_send, gx_recv,
    b1_send, b1_recv, b2_send, b2_recv, b3_send, b3_recv, b4_send, b4_recv, b5_send, b5_recv,
    b6_send, b6_recv, at_send, at_recv,
    e1_send, e1_recv, e2_send, e2_recv, q0_send, q0_recv, q1_send, q1_recv,
    q2_send, q2_recv, q3_send, q3_recv, a_send, a_recv,
):
    f = lax.axis_index("fem")
    r = lax.axis_index("row")
    c = lax.axis_index("col")
    zh, y = f // 4, f % 4
    zl, core = c // 2, c % 2
    z = zh * 2 + zl
    three = (1, 2, 3)
    recv = (recv0, recv1, recv2, recv3)

    def at_y(d):
        return (zh * 4 + (y + d) % 4, r, c)

    def at_z(d):
        to = (z + d) % 8
        return ((to // 2) * 4 + y, r, (to % 2) * 2 + core)

    def at_zh(d):
        return (((zh + d) % 4) * 4 + y, r, c)

    def at_x(d):
        return (f, (r + d) % 4, c)

    def at_col(d):
        return (f, r, (c + d) % 4)

    partner = (f, r, c + 1 - 2 * core)

    def copy(src, dst, send, recv_sem, to):
        return pltpu.make_async_remote_copy(
            src_ref=src, dst_ref=dst, send_sem=send, recv_sem=recv_sem,
            device_id=to, device_id_type=MESH,
        )

    def arrive(dst, recv_sem):
        copy(dst, dst, recv_sem, recv_sem, at_x(1)).wait_recv()

    def start(copies):
        for one in copies:
            one.start()

    def rows_of(index, count):
        return pl.ds(pl.multiple_of(index * count, count), count)

    barrier = pltpu.get_barrier_semaphore()
    greet = [at_y(d) for d in three] + [at_z(d) for d in range(1, 8)]
    greet += [at_x(d) for d in three] + [at_col(d) for d in three]
    for to in greet:
        pl.semaphore_signal(barrier, inc=1, device_id=to, device_id_type=MESH)
    pl.semaphore_wait(barrier, len(greet))

    in_panel = r < 2
    is_root = (f == 0) & in_panel
    mine = r % 2

    b1 = [
        copy(
            dense_ref.at[0, :, rows_of((y + d) % 4, 32)], prow.at[d - 1],
            b1_send.at[d - 1], b1_recv.at[d - 1], at_y(d),
        )
        for d in three
    ]
    e1 = [
        copy(
            bem_ref.at[pl.ds(d * 32, 32), pl.ds(0, 256)], dy32, e1_send.at[d - 1], e1_recv,
            (d, r, c),
        )
        for d in three
    ]
    e2 = [
        copy(
            dy32.at[rows_of((zh + d) % 4, 8)], d8, e2_send.at[d - 1], e2_recv, at_zh(d)
        )
        for d in three
    ]
    a_copies = [
        copy(bem_ref.at[:, pl.ds(0, 256)], cols, a_send.at[d - 1], a_recv, at_col(d))
        for d in three
    ]
    px = [
        copy(
            bem_ref.at[:, rows_of((r + d) % 4, 512)], xpart.at[mine],
            px_send.at[d - 1], px_recv.at[mine], at_x(d),
        )
        for d in three
    ]

    @pl.when(in_panel)
    def _():
        start(b1)

        @pl.when(f == 0)
        def _():
            @pl.when(c == 0)
            def _():
                start(e1)
                dy32[...] = bem_ref[0:32, 0:256]

            start(px)
            xpart[mine] = bem_ref[:, rows_of(mine, 512)]

    @pl.when(c == 0)
    def _():
        start(a_copies)
        cols[...] = bem_ref[:, 0:256]

    rounds = (2, 1, 3, 0)
    tile_row = [(zh + turn) % 4 for turn in rounds]
    y_copies = [
        [
            copy(
                dense_ref.at[tile_row[k] * 4 + (y + d) % 4], recv[k].at[d - 1],
                y_send.at[d - 1, k], y_recv.at[d - 1, k], at_y(d),
            )
            for d in three
        ]
        for k in range(4)
    ]
    start(y_copies[0])

    b2 = copy(psum.at[1], pother, b2_send, b2_recv, partner)
    b3 = [
        copy(
            psum.at[0, ((z + d) % 8) % 2, rows_of(((z + d) % 8) // 2, 8)], pz.at[d - 1],
            b3_send.at[d - 1], b3_recv.at[d - 1], at_z(d),
        )
        for d in range(1, 8)
    ]

    @pl.when(in_panel & (c == 0))
    def _():
        @pl.when(zh == 0)
        def _():
            @pl.when(y != 0)
            def _():
                arrive(dy32, e1_recv)

            start(e2)
            d8[...] = dy32[0:8]

    @pl.when(in_panel)
    def _():
        for one in b1:
            one.wait_recv()

        def add_row(b4, carry):
            for i in range(4):
                b = b4 * 4 + i
                total = (
                    dense_ref[0, slot_ref[b], rows_of(y, 32)].astype(F32) * weight_ref[b]
                )
                for d in three:
                    total += (
                        prow[d - 1, slot_ref[d * 16 + b]].astype(F32) * weight_ref[d * 16 + b]
                    )
                psum[(b4 % 2 + core) % 2, b4 // 2, :, i * T : (i + 1) * T] = total
            return carry

        lax.fori_loop(0, 4, add_row, 0)
        b2.start()

    py = [
        copy(xpart.at[:, pl.ds(d * 32, 32)], ypart, py_send.at[d - 1], py_recv, (d, r, c))
        for d in three
    ]
    pzs = [copy(ypart, ypart, pz_send.at[d - 1], pz_recv, at_zh(d)) for d in three]

    @pl.when(f == 0)
    def _():
        for m in range(2):
            @pl.when(r != m)
            def _():
                arrive(xpart.at[m], px_recv.at[m])

        start(py)
        ypart[...] = xpart[:, 0:32]

    @pl.when(in_panel)
    def _():
        b2.wait_recv()
        psum[0] = psum[0] + pother[...]
        start(b3)

    start(y_copies[1])

    @pl.when(zh == 0)
    def _():
        @pl.when(y != 0)
        def _():
            arrive(ypart, py_recv)

        start(pzs)

    q0 = [copy(gq.at[mine], gq.at[mine], q0_send.at[d - 1], q0_recv, at_col(d)) for d in three]
    q1 = [
        copy(gq.at[mine], gq.at[mine], q1_send.at[d - 1], q1_recv.at[mine], at_x(d))
        for d in three
    ]
    b4 = [
        copy(piece, pa32.at[rows_of(zh, 8)], b4_send.at[d - 1], b4_recv.at[d - 1], at_zh(d))
        for d in three
    ]

    @pl.when(in_panel)
    def _():
        for one in b3:
            one.wait_recv()
        total = psum[0, zl, rows_of(zh, 8)]
        for d in range(7):
            total += pz[d]
        piece[...] = total
        start(b4)
        pa32[rows_of(zh, 8)] = total

        @pl.when(c == 0)
        def _():
            @pl.when(zh != 0)
            def _():
                arrive(d8, e2_recv)

            for m in range(2):
                @pl.when(r == m)
                def _():
                    gq[m, :, (1 - m) * T : (2 - m) * T] = d8[:, (1 - m) * T : (2 - m) * T]
                    gq[m, :, m * T : (m + 1) * T] = d8[:, m * T : (m + 1) * T] + total[:, 0:T]

            start(q0)

        @pl.when(c != 0)
        def _():
            arrive(gq.at[mine], q0_recv)

        start(q1)

    q2 = [
        copy(gq, g32.at[:, rows_of(zh, 8)], q2_send.at[d - 1], q2_recv.at[d - 1], at_zh(d))
        for d in three
    ]
    q3 = [
        copy(g32, diag.at[:, rows_of(y, 32)], q3_send.at[d - 1], q3_recv.at[d - 1], at_y(d))
        for d in three
    ]
    b5 = [
        copy(pa32, pa.at[mine, rows_of(y, 32)], b5_send.at[d - 1], b5_recv.at[d - 1], at_y(d))
        for d in three
    ]
    b6 = [
        copy(pa.at[mine], pa.at[mine], b6_send.at[d - 1], b6_recv.at[mine], at_x(d))
        for d in three
    ]
    tile_lanes = rows_of(f % 4, T)
    at_copies = [
        copy(pa.at[mine, :, tile_lanes], atile, at_send.at[d - 1], at_recv, at_col(d))
        for d in three
    ]
    for m in range(2):
        @pl.when(r != m)
        def _():
            arrive(gq.at[m], q1_recv.at[m])

    start(q2)
    g32[:, rows_of(zh, 8)] = gq[...]

    @pl.when(in_panel)
    def _():
        for one in b4:
            one.wait_recv()
        start(b5)
        pa[mine, rows_of(y, 32)] = pa32[...]

    for one in q2:
        one.wait_recv()
    start(q3)
    diag[:, rows_of(y, 32)] = g32[...]

    gy = [
        copy(ypart, zpart.at[:, rows_of(y, 32)], gy_send.at[d - 1], gy_recv.at[d - 1], at_y(d))
        for d in three
    ]
    gx = [
        copy(zpart, panel.at[r], gx_send.at[d - 1], gx_recv.at[d - 1], at_x(d)) for d in three
    ]

    @pl.when(zh != 0)
    def _():
        arrive(ypart, pz_recv)

    start(gy)
    zpart[:, rows_of(y, 32)] = ypart[...]

    swaps = [
        copy(
            acc.at[1, rows_of(tile_row[k], 2)], other.at[rows_of(tile_row[k], 2)],
            c_send.at[k], c_recv.at[k], partner,
        )
        for k in range(4)
    ]

    def add_round(k):
        for one in y_copies[k]:
            one.wait_recv()
        q = tile_row[k]

        def gather(b4, carry):
            for i in range(4):
                b = b4 * 4 + i
                total = dense_ref[q * 4 + y, slot_ref[b]].astype(F32) * weight_ref[b]
                for d in three:
                    total += (
                        recv[k][d - 1, slot_ref[d * 16 + b]].astype(F32) * weight_ref[d * 16 + b]
                    )
                acc[(b4 % 2 + core) % 2, q * 2 + b4 // 2, :, i * T : (i + 1) * T] = total
            return carry

        lax.fori_loop(0, 4, gather, 0)
        swaps[k].start()

    half = T // 2
    ring = []

    def hop(src, dst, lane, d):
        one = copy(src, dst, r_send.at[lane, d], r_recv.at[lane, d], at_z(1 + 6 * lane))
        one.start()
        ring.append(one)
        return one

    def first_hop():
        swaps[0].wait_recv()
        far = (z + 4) % 8
        acc[0, far] = acc[0, far] + other[far]
        return (
            hop(acc.at[0, far, pl.ds(0, half)], plus0, 0, 0),
            hop(acc.at[0, far, pl.ds(half, half)], minus0, 1, 0),
        )

    def next_hop(d, up, down):
        zp = (z + d) % 8
        zm = (z + 8 - d) % 8
        acc[0, zp] = acc[0, zp] + other[zp]
        acc[0, zm] = acc[0, zm] + other[zm]
        up.wait_recv()
        if d == 3:
            acc[0, zp, 0:half] = acc[0, zp, 0:half] + plus0[...]
        else:
            acc[0, zp] = acc[0, zp] + plus[2 - d]
        up = hop(acc.at[0, zp], plus.at[3 - d], 0, 4 - d)
        down.wait_recv()
        if d == 3:
            acc[0, zm, half:T] = acc[0, zm, half:T] + minus0[...]
        else:
            acc[0, zm] = acc[0, zm] + minus[2 - d]
        down = hop(acc.at[0, zm], minus.at[3 - d], 1, 4 - d)
        return up, down

    add_round(0)

    @pl.when(in_panel)
    def _():
        for one in b5:
            one.wait_recv()
        start(b6)

        @pl.when(c == f // 4)
        def _():
            start(at_copies)
            atile[...] = pa[mine, :, tile_lanes]

    start(y_copies[2])
    for one in gy:
        one.wait_recv()
    start(gx)
    panel[r] = zpart[...]
    for one in q3:
        one.wait_recv()

    @pl.when(c != 0)
    def _():
        arrive(cols, a_recv)

    @pl.when(in_panel)
    def _():
        @pl.when(c != f // 4)
        def _():
            arrive(atile, at_recv)

        turned = atile[...].T
        for m in range(2):
            @pl.when(r == m)
            def _():
                cols[:, m * T : (m + 1) * T] = cols[:, m * T : (m + 1) * T] + turned

    identity = (
        lax.broadcasted_iota(jnp.int32, (T, T), 0) == lax.broadcasted_iota(jnp.int32, (T, T), 1)
    ).astype(F32)
    work[0:T, :] = diag[0, :, 0:T]
    work[T : 2 * T, :] = diag[1, :, 0:T]
    work[2 * T : 3 * T, :] = cols[:, 0:T]
    unit[...] = identity
    eliminate_part(work, unit, 0, 3 * T)
    up, down = first_hop()
    eliminate_part(work, unit, 1, 3 * T)
    start(y_copies[3])
    add_round(1)
    eliminate_part(work, unit, 2, 3 * T)
    eliminate_part(work, unit, 3, 3 * T)
    turn_back(work)
    first = work[...]
    first_inv = unit[...]
    upper = highest(first_inv, diag[0, :, T:256])
    add_round(2)
    swaps[1].wait_recv()
    swaps[2].wait_recv()
    up, down = next_hop(3, up, down)
    work[0:T, :] = diag[1, :, T:256] - highest(first[T : 2 * T], upper)
    work[T : 2 * T, :] = cols[:, T:256] - highest(first[2 * T :], upper)
    unit[...] = identity
    eliminate_part(work, unit, 0, 2 * T)
    eliminate_part(work, unit, 1, 2 * T)
    up, down = next_hop(2, up, down)
    eliminate_part(work, unit, 2, 2 * T)
    add_round(3)
    eliminate_part(work, unit, 3, 2 * T)
    turn_back(work)
    swaps[3].wait_recv()
    up, down = next_hop(1, up, down)

    second = work[0 : 2 * T, :]
    second_inv = unit[...]
    corner = -highest(second_inv, highest(first[T : 2 * T], first_inv))
    lower = second[T:]
    left = jnp.where(
        is_root,
        jnp.where(r == 0, first_inv, corner),
        -(highest(first[2 * T :], first_inv) + highest(lower, corner)),
    )
    right = jnp.where(
        is_root,
        jnp.where(r == 0, jnp.zeros_like(second_inv), second_inv),
        -highest(lower, second_inv),
    )
    keep = jnp.where(is_root, 0.0, 1.0).astype(F32)
    for one in gx:
        one.wait_recv()
    for m in range(2):
        @pl.when(r != m)
        def _():
            arrive(pa.at[m], b6_recv.at[m])

    for n in range(4):
        for m in range(2):
            panel[n, m, :, m * T : (m + 1) * T] = (
                panel[n, m, :, m * T : (m + 1) * T] + pa[m, :, n * T : (n + 1) * T]
            )
    for n in range(4):
        cut = pl.ds(n * 512, 512)
        out_ref[:, cut] = (
            bem_ref[:, cut] * keep + highest(left, panel[n, 0]) + highest(right, panel[n, 1])
        )

    up.wait_recv()
    down.wait_recv()
    for i in range(4):
        lanes = pl.ds(pl.multiple_of((i * 4 + r) * T, T), T)
        part = pl.ds(i * T, T)
        out_ref[:, lanes] = out_ref[:, lanes] + keep * (
            acc[0, z, :, part] + other[z, :, part] + plus[2, :, part] + minus[2, :, part]
        )

    @pl.when(c == 0)
    def _():
        out_ref[:, 0:T] = jnp.where(
            is_root, jnp.where(r == 0, first[0:T], first[T : 2 * T]), first[2 * T :]
        )
        out_ref[:, T:256] = jnp.where(
            is_root, jnp.where(r == 0, upper, second[0:T]), lower
        )

    def sent(copies):
        for one in copies:
            one.wait_send()

    sent(ring + swaps + gy + gx + q2 + q3)
    for k in range(4):
        sent(y_copies[k])

    @pl.when(in_panel)
    def _():
        sent(b1 + [b2] + b3 + b4 + b5 + b6 + q1)

        @pl.when(c == 0)
        def _():
            sent(q0)

            @pl.when(zh == 0)
            def _():
                sent(e2)

        @pl.when(f == 0)
        def _():
            sent(px)

            @pl.when(c == 0)
            def _():
                sent(e1)

        @pl.when(c == f // 4)
        def _():
            sent(at_copies)

    @pl.when(c == 0)
    def _():
        sent(a_copies)

    @pl.when(f == 0)
    def _():
        sent(py)

    @pl.when(zh == 0)
    def _():
        sent(pzs)


def solve(slots, weights, dense, bem):
    vmem = pl.BlockSpec(memory_space=pltpu.VMEM)
    smem = pl.BlockSpec(memory_space=pltpu.SMEM)
    dma = pltpu.SemaphoreType.DMA
    f32 = lambda *shape: pltpu.VMEM(shape, F32)
    return pl.pallas_call(
        solve_kernel,
        out_shape=jax.ShapeDtypeStruct(bem.shape, F32),
        in_specs=[smem, smem, vmem, vmem],
        out_specs=vmem,
        scratch_shapes=[
            *[pltpu.VMEM((3, 8, T, T), BF16)] * 4,
            f32(2, 8, T, 512),
            f32(8, T, 512),
            f32(T // 2, 512), f32(T // 2, 512), f32(3, T, 512), f32(3, T, 512),
            f32(2, T, 512), f32(2, 32, 512), f32(2, T, 512), f32(4, 2, T, 512),
            pltpu.VMEM((3, 8, 32, T), BF16),
            f32(2, 2, 32, 512), f32(2, 32, 512), f32(7, 8, 512), f32(8, 512), f32(32, 512),
            f32(2, T, 512), f32(T, T),
            f32(32, 256), f32(8, 256), f32(2, 8, 256), f32(2, 32, 256), f32(2, T, 256),
            f32(T, 256),
            f32(3 * T, T), f32(T, T),
            dma((3, 4)), dma((3, 4)), dma((4,)), dma((4,)), dma((2, 4)), dma((2, 4)),
            dma((3,)), dma((2,)), dma((3,)), dma, dma((3,)), dma,
            dma((3,)), dma((3,)), dma((3,)), dma((3,)),
            dma((3,)), dma((3,)), dma, dma, dma((7,)), dma((7,)), dma((3,)), dma((3,)),
            dma((3,)), dma((3,)),
            dma((3,)), dma((2,)), dma((3,)), dma,
            dma((3,)), dma, dma((3,)), dma, dma((3,)), dma, dma((3,)), dma((2,)),
            dma((3,)), dma((3,)), dma((3,)), dma((3,)), dma((3,)), dma,
        ],
        compiler_params=pltpu.CompilerParams(
            collective_id=0, has_side_effects=True, vmem_limit_bytes=VMEM_LIMIT
        ),
        name="solve",
    )(slots, weights, dense, bem)


def local(inverse_factor, coupling, boundary_tiles, bem_block):
    tiles = lax.axis_size("fem")
    dense, slots, weights = contribution(boundary_tiles, inverse_factor[0], coupling[0], tiles)
    return solve(slots, weights, dense, bem_block[0, 0])[None, None]


def solution(mesh):
    placed = (
        P(("fem", "row", "col"), None, None),
        P(("fem", "row", "col"), None, None),
        P(),
        P(None, ("fem", "row"), None, "col"),
    )
    return jax.shard_map(
        local,
        mesh=mesh,
        in_specs=placed,
        out_specs=P(None, ("fem", "row"), None, "col"),
        check_vma=False,
    )
```

time: 1600 us -> 123 us (0.08)
  waiting for transfers between devices: 960 us -> 0 us
  local copies, waits for them, and re-layouts: 250 us -> 3.78 us
  other arithmetic: 194 us -> 0 us
  matrix products: 152 us -> 0 us
  Pallas kernels: 0 us -> 119 us
    psum x2 -> x0, waiting for transfers between devices: 778 us -> none  [broadcast(): return lax.psum(jnp.where(mine, value, jnp.zeros_like(value)), axis)]
    dynamic_slice x481 -> x0, local copies, waits for them, and re-layouts: 190 us -> none  [the longest x240 145 us: sweep(): pivot = current[column, column]]
    all_to_all x1 -> x0, waiting for transfers between devices: 182 us -> none  [local(): lax.all_to_all(placed, ('fem', 'col'), split_axis=0, concat_axis=0, tiled...]
    broadcast_in_dim x240 -> x0, other arithmetic: 153 us -> none  [sweep(): jnp.where(below[:, None] & (places == column)[None, :], scaled[:, None],...]
    dot_general x303 -> x0, matrix products: 152 us -> none  [the longest x300 119 us: highest(): return jnp.dot(left, right, precision=lax.Precision.HIGHEST)]
    pallas_call x0 -> x2, Pallas kernels: none -> 119 us  [the longest x1 107 us: solve(): pl.pallas_call(solve_kernel, out_shape=jax.ShapeDtypeStruct(bem.shape, F3...]
    sub x240 -> x0, other arithmetic: 18.4 us -> none  [sweep(): current - jnp.where(trailing, scaled[:, None] * row_values[None, :], 0.0)]
  transfers between devices with their start and end apart: 3 -> 0, of which waited for: 3 -> 0; matrix products, arithmetic and copies ran while one was open for 0% -> 0% of each run, Pallas kernels for 0% -> 0%
where the time goes in v2:
time: 123 us
  Pallas kernels  119 us (97%)
  local copies, waits for them, and re-layouts  3.78 us (3%)
    pallas_call x1, Pallas kernels, solve(): pl.pallas_call(solve_kernel, out_shape=jax.ShapeDtypeStruct(bem.shape, F3...  107 us
    pallas_call x1, Pallas kernels, contribution(): pl.pallas_call(contribution_kernel, out_shape=[jax.ShapeDtypeStruct((tile...  12.1 us
    unnamed x2, local copies, waits for them, and re-layouts  3.78 us

profile of v2, /device:TPU:1, one launch (start us, length us, event | category | flops | bytes accessed | tf_op | source)
XLA Modules:
  0.0 122.7 jit_solution(14929637671847185824)
XLA Ops:
  0.0 1.5 %copy.5.tiles_ref = s32[256,8]{1,0:T(8,128)} copy(s32[256,8]{0,1:T(8,128)} %param.6) | data formatting | bytes 16384 | tf_op args[2]
  1.5 12.1 %contribution.1 = (bf16[16,8,128,128]{3,2,1,0:T(8,128)(2,1)}, s32[64]{0:T(128)}, f32[64]{0:T(128)}) custom-call(s32[256,8]{1,0:T(8,128)} %copy.5.tiles_ref, bf16[1536,1536]{1,0:T(8,128)(2,1)} %bitcast.4, bf16[1536,1024]{1,0:T(8,128)(2,1)} %bitcast.6), custom_call_target="tpu_custom_call" | custom-call | tf_op jit(solution)/shard_map/contribution/pallas_call | solution.py:67
  13.6 106.8 %solve.1 = f32[128,2048]{1,0:T(8,128)} custom-call(s32[64]{0:T(128)} %get-tuple-element.8.slot_ref, f32[64]{0:T(128)} %get-tuple-element.9.weight_ref, bf16[16,8,128,128]{3,2,1,0:T(8,128)(2,1)} %get-tuple-element.10.dense_ref, f32[128,2048]{1,0:T(8,128)} %bitcast.7), custom_call_target="tpu_custom_call" | custom-call | tf_op jit(solution)/shard_map/solve/pallas_call | solution.py:653
  120.4 2.3 %copy.7 = f32[1,1,128,2048]{3,2,1,0:T(8,128)} copy(f32[1,1,128,2048]{3,2,1,0:T(8,128)} %bitcast.5) | data formatting | bytes 2097152

commit v3 on v2

--- a/solution.py
+++ b/solution.py
@@ -14,69 +14,6 @@
 
 def highest(left, right):
     return jnp.dot(left, right, precision=lax.Precision.HIGHEST, preferred_element_type=F32)
-
-
-def contribution_kernel(
-    tiles_ref, factor_ref, coupling_ref, out_ref, slot_ref, weight_ref, coupled
-):
-    f = lax.axis_index("fem")
-    r = lax.axis_index("row")
-    c = lax.axis_index("col")
-    order, width = coupling_ref.shape
-    tiles, slots = out_ref.shape[0], out_ref.shape[1]
-    step = 256
-    for i in range(4 * tiles):
-        slot_ref[i] = 0
-        weight_ref[i] = 0.0
-    for d in range(4):
-        source = (((f // 4) * 4 + (f + 4 - d) % 4) * 4 + r) * 4 + c
-        for k in range(slots):
-            tile = tiles_ref[source, k]
-            slot_ref[d * tiles + tile] = k
-            weight_ref[d * tiles + tile] = 1.0
-    me = (f * 4 + r) * 4 + c
-    out_ref[...] = jnp.zeros_like(out_ref)
-    for i in range(order // step):
-        for n in range(width // 512):
-            coupled[i * step : (i + 1) * step, n * 512 : (n + 1) * 512] = jnp.dot(
-                factor_ref[i * step : (i + 1) * step, : (i + 1) * step],
-                coupling_ref[: (i + 1) * step, n * 512 : (n + 1) * 512],
-                preferred_element_type=F32,
-            ).astype(BF16)
-    for pair in range(width // step):
-        for n in range(width // 512):
-            block = lax.dot_general(
-                coupled[:, pair * step : (pair + 1) * step],
-                coupled[:, n * 512 : (n + 1) * 512],
-                (((0,), (0,)), ((), ())),
-                preferred_element_type=F32,
-            ).astype(BF16)
-            for half in range(step // T):
-                place = tiles_ref[me, pair * (step // T) + half]
-                for j in range(512 // T):
-                    out_ref[place, n * (512 // T) + j] = block[
-                        half * T : (half + 1) * T, j * T : (j + 1) * T
-                    ]
-
-
-def contribution(boundary_tiles, factor, coupling, tiles):
-    order, width = coupling.shape
-    slots = width // T
-    smem = pl.BlockSpec(memory_space=pltpu.SMEM)
-    vmem = pl.BlockSpec(memory_space=pltpu.VMEM)
-    return pl.pallas_call(
-        contribution_kernel,
-        out_shape=[
-            jax.ShapeDtypeStruct((tiles, slots, T, T), BF16),
-            jax.ShapeDtypeStruct((4 * tiles,), jnp.int32),
-            jax.ShapeDtypeStruct((4 * tiles,), F32),
-        ],
-        in_specs=[smem, vmem, vmem],
-        out_specs=[vmem, smem, smem],
-        scratch_shapes=[pltpu.VMEM((order, width), BF16)],
-        compiler_params=pltpu.CompilerParams(vmem_limit_bytes=VMEM_LIMIT),
-        name="contribution",
-    )(boundary_tiles, factor, coupling)
 
 
 def eliminate_part(work, unit, part, last):
@@ -110,8 +47,9 @@
 
 
 def solve_kernel(
-    slot_ref, weight_ref, dense_ref, bem_ref,
+    tiles_ref, factor_ref, coupling_ref, bem_ref,
     out_ref,
+    slot_ref, weight_ref, factor, coupling, coupled, compact, dense_ref, f_sem, k_sem,
     recv0, recv1, recv2, recv3, acc, other, plus0, minus0, plus, minus,
     xpart, ypart, zpart, panel,
     prow, psum, pother, pz, piece, pa32, pa, atile,
@@ -167,6 +105,22 @@
     def rows_of(index, count):
         return pl.ds(pl.multiple_of(index * count, count), count)
 
+    order, width = coupling.shape
+    step = 256
+    loads = []
+    for i in range(order // step):
+        block = pl.ds(i * step, step)
+        left_part = pl.ds(0, (i + 1) * step)
+        loads.append(
+            (
+                pltpu.make_async_copy(
+                    factor_ref.at[block, left_part], factor.at[block, left_part], f_sem.at[i]
+                ),
+                pltpu.make_async_copy(coupling_ref.at[block], coupling.at[block], k_sem.at[i]),
+            )
+        )
+        start(loads[i])
+
     barrier = pltpu.get_barrier_semaphore()
     greet = [at_y(d) for d in three] + [at_z(d) for d in range(1, 8)]
     greet += [at_x(d) for d in three] + [at_col(d) for d in three]
@@ -210,19 +164,15 @@
         for d in three
     ]
 
-    @pl.when(in_panel)
-    def _():
-        start(b1)
-
-        @pl.when(f == 0)
-        def _():
-            @pl.when(c == 0)
-            def _():
-                start(e1)
-                dy32[...] = bem_ref[0:32, 0:256]
-
-            start(px)
-            xpart[mine] = bem_ref[:, rows_of(mine, 512)]
+    @pl.when(is_root)
+    def _():
+        @pl.when(c == 0)
+        def _():
+            start(e1)
+            dy32[...] = bem_ref[0:32, 0:256]
+
+        start(px)
+        xpart[mine] = bem_ref[:, rows_of(mine, 512)]
 
     @pl.when(c == 0)
     def _():
@@ -241,7 +191,101 @@
         ]
         for k in range(4)
     ]
+
+    py = [
+        copy(xpart.at[:, pl.ds(d * 32, 32)], ypart, py_send.at[d - 1], py_recv, (d, r, c))
+        for d in three
+    ]
+    pzs = [copy(ypart, ypart, pz_send.at[d - 1], pz_recv, at_zh(d)) for d in three]
+
+    gy = [
+        copy(ypart, zpart.at[:, rows_of(y, 32)], gy_send.at[d - 1], gy_recv.at[d - 1], at_y(d))
+        for d in three
+    ]
+    gx = [
+        copy(zpart, panel.at[r], gx_send.at[d - 1], gx_recv.at[d - 1], at_x(d)) for d in three
+    ]
+
+    for d in range(4):
+        source = ((zh * 4 + (y + 4 - d) % 4) * 4 + r) * 4 + c
+        listed = [tiles_ref[source, k] for k in range(8)]
+
+        def look(b, carry):
+            slot = jnp.int32(0)
+            weight = jnp.float32(0.0)
+            for k in range(8):
+                slot = jnp.where(listed[k] == b, k, slot)
+                weight = jnp.where(listed[k] == b, jnp.float32(1.0), weight)
+            slot_ref[d * 16 + b] = slot
+            weight_ref[d * 16 + b] = weight
+            return carry
+
+        lax.fori_loop(0, 16, look, 0)
+
+    for i in range(order // step):
+        for one in loads[i]:
+            one.wait()
+        for n in range(width // 512):
+            coupled[i * step : (i + 1) * step, n * 512 : (n + 1) * 512] = jnp.dot(
+                factor[i * step : (i + 1) * step, : (i + 1) * step],
+                coupling[: (i + 1) * step, n * 512 : (n + 1) * 512],
+                preferred_element_type=F32,
+            ).astype(BF16)
+
+    @pl.when(in_panel & (c == 0))
+    def _():
+        @pl.when(zh == 0)
+        def _():
+            @pl.when(y != 0)
+            def _():
+                arrive(dy32, e1_recv)
+
+            start(e2)
+            d8[...] = dy32[0:8]
+
+    @pl.when(f == 0)
+    def _():
+        for m in range(2):
+            @pl.when(r != m)
+            def _():
+                arrive(xpart.at[m], px_recv.at[m])
+
+        start(py)
+        ypart[...] = xpart[:, 0:32]
+
+    for pair in range(width // step):
+        for n in range(width // 512):
+            both = lax.dot_general(
+                coupled[:, pair * step : (pair + 1) * step],
+                coupled[:, n * 512 : (n + 1) * 512],
+                (((0,), (0,)), ((), ())),
+                preferred_element_type=F32,
+            ).astype(BF16)
+            for i in range(step // T):
+                for j in range(512 // T):
+                    compact[pair * (step // T) + i, n * (512 // T) + j] = both[
+                        i * T : (i + 1) * T, j * T : (j + 1) * T
+                    ]
+
+    dense_ref[0] = compact[slot_ref[0]]
+
+    @pl.when(in_panel)
+    def _():
+        start(b1)
+
+    def place(b, carry):
+        dense_ref[b] = compact[slot_ref[b]]
+        return carry
+
+    lax.fori_loop(1, 16, place, 0)
     start(y_copies[0])
+    @pl.when(zh == 0)
+    def _():
+        @pl.when(y != 0)
+        def _():
+            arrive(ypart, py_recv)
+
+        start(pzs)
 
     b2 = copy(psum.at[1], pother, b2_send, b2_recv, partner)
     b3 = [
@@ -252,17 +296,6 @@
         for d in range(1, 8)
     ]
 
-    @pl.when(in_panel & (c == 0))
-    def _():
-        @pl.when(zh == 0)
-        def _():
-            @pl.when(y != 0)
-            def _():
-                arrive(dy32, e1_recv)
-
-            start(e2)
-            d8[...] = dy32[0:8]
-
     @pl.when(in_panel)
     def _():
         for one in b1:
@@ -271,12 +304,12 @@
         def add_row(b4, carry):
             for i in range(4):
                 b = b4 * 4 + i
-                total = (
-                    dense_ref[0, slot_ref[b], rows_of(y, 32)].astype(F32) * weight_ref[b]
+                total = compact[slot_ref[0], slot_ref[b], rows_of(y, 32)].astype(F32) * (
+                    weight_ref[b] * weight_ref[0]
                 )
                 for d in three:
-                    total += (
-                        prow[d - 1, slot_ref[d * 16 + b]].astype(F32) * weight_ref[d * 16 + b]
+                    total += prow[d - 1, slot_ref[d * 16 + b]].astype(F32) * (
+                        weight_ref[d * 16 + b] * weight_ref[d * 16]
                     )
                 psum[(b4 % 2 + core) % 2, b4 // 2, :, i * T : (i + 1) * T] = total
             return carry
@@ -284,22 +317,6 @@
         lax.fori_loop(0, 4, add_row, 0)
         b2.start()
 
-    py = [
-        copy(xpart.at[:, pl.ds(d * 32, 32)], ypart, py_send.at[d - 1], py_recv, (d, r, c))
-        for d in three
-    ]
-    pzs = [copy(ypart, ypart, pz_send.at[d - 1], pz_recv, at_zh(d)) for d in three]
-
-    @pl.when(f == 0)
-    def _():
-        for m in range(2):
-            @pl.when(r != m)
-            def _():
-                arrive(xpart.at[m], px_recv.at[m])
-
-        start(py)
-        ypart[...] = xpart[:, 0:32]
-
     @pl.when(in_panel)
     def _():
         b2.wait_recv()
@@ -307,14 +324,13 @@
         start(b3)
 
     start(y_copies[1])
-
-    @pl.when(zh == 0)
-    def _():
-        @pl.when(y != 0)
-        def _():
-            arrive(ypart, py_recv)
-
-        start(pzs)
+    @pl.when(zh != 0)
+    def _():
+        arrive(ypart, pz_recv)
+
+    start(gy)
+    zpart[:, rows_of(y, 32)] = ypart[...]
+
 
     q0 = [copy(gq.at[mine], gq.at[mine], q0_send.at[d - 1], q0_recv, at_col(d)) for d in three]
     q1 = [
@@ -397,21 +413,11 @@
         one.wait_recv()
     start(q3)
     diag[:, rows_of(y, 32)] = g32[...]
-
-    gy = [
-        copy(ypart, zpart.at[:, rows_of(y, 32)], gy_send.at[d - 1], gy_recv.at[d - 1], at_y(d))
-        for d in three
-    ]
-    gx = [
-        copy(zpart, panel.at[r], gx_send.at[d - 1], gx_recv.at[d - 1], at_x(d)) for d in three
-    ]
-
-    @pl.when(zh != 0)
-    def _():
-        arrive(ypart, pz_recv)
-
-    start(gy)
-    zpart[:, rows_of(y, 32)] = ypart[...]
+    start(y_copies[2])
+    for one in gy:
+        one.wait_recv()
+    start(gx)
+    panel[r] = zpart[...]
 
     swaps = [
         copy(
@@ -425,14 +431,17 @@
         for one in y_copies[k]:
             one.wait_recv()
         q = tile_row[k]
+        row = q * 4 + y
 
         def gather(b4, carry):
             for i in range(4):
                 b = b4 * 4 + i
-                total = dense_ref[q * 4 + y, slot_ref[b]].astype(F32) * weight_ref[b]
+                total = compact[slot_ref[row], slot_ref[b]].astype(F32) * (
+                    weight_ref[b] * weight_ref[row]
+                )
                 for d in three:
-                    total += (
-                        recv[k][d - 1, slot_ref[d * 16 + b]].astype(F32) * weight_ref[d * 16 + b]
+                    total += recv[k][d - 1, slot_ref[d * 16 + b]].astype(F32) * (
+                        weight_ref[d * 16 + b] * weight_ref[d * 16 + row]
                     )
                 acc[(b4 % 2 + core) % 2, q * 2 + b4 // 2, :, i * T : (i + 1) * T] = total
             return carry
@@ -490,11 +499,6 @@
             start(at_copies)
             atile[...] = pa[mine, :, tile_lanes]
 
-    start(y_copies[2])
-    for one in gy:
-        one.wait_recv()
-    start(gx)
-    panel[r] = zpart[...]
     for one in q3:
         one.wait_recv()
 
@@ -513,6 +517,8 @@
             @pl.when(r == m)
             def _():
                 cols[:, m * T : (m + 1) * T] = cols[:, m * T : (m + 1) * T] + turned
+
+    start(y_copies[3])
 
     identity = (
         lax.broadcasted_iota(jnp.int32, (T, T), 0) == lax.broadcasted_iota(jnp.int32, (T, T), 1)
@@ -524,7 +530,6 @@
     eliminate_part(work, unit, 0, 3 * T)
     up, down = first_hop()
     eliminate_part(work, unit, 1, 3 * T)
-    start(y_copies[3])
     add_round(1)
     eliminate_part(work, unit, 2, 3 * T)
     eliminate_part(work, unit, 3, 3 * T)
@@ -645,7 +650,7 @@
         sent(pzs)
 
 
-def solve(slots, weights, dense, bem):
+def solve(tiles, factor, coupling, bem):
     vmem = pl.BlockSpec(memory_space=pltpu.VMEM)
     smem = pl.BlockSpec(memory_space=pltpu.SMEM)
     dma = pltpu.SemaphoreType.DMA
@@ -653,9 +658,14 @@
     return pl.pallas_call(
         solve_kernel,
         out_shape=jax.ShapeDtypeStruct(bem.shape, F32),
-        in_specs=[smem, smem, vmem, vmem],
+        in_specs=[smem, pl.BlockSpec(memory_space=pl.ANY), pl.BlockSpec(memory_space=pl.ANY), vmem],
         out_specs=vmem,
         scratch_shapes=[
+            pltpu.SMEM((64,), jnp.int32), pltpu.SMEM((64,), F32),
+            pltpu.VMEM(factor.shape, BF16), pltpu.VMEM(coupling.shape, BF16),
+            pltpu.VMEM(coupling.shape, BF16),
+            pltpu.VMEM((8, 8, T, T), BF16), pltpu.VMEM((16, 8, T, T), BF16),
+            dma((6,)), dma((6,)),
             *[pltpu.VMEM((3, 8, T, T), BF16)] * 4,
             f32(2, 8, T, 512),
             f32(8, T, 512),
@@ -680,13 +690,11 @@
             collective_id=0, has_side_effects=True, vmem_limit_bytes=VMEM_LIMIT
         ),
         name="solve",
-    )(slots, weights, dense, bem)
+    )(tiles, factor, coupling, bem)
 
 
 def local(inverse_factor, coupling, boundary_tiles, bem_block):
-    tiles = lax.axis_size("fem")
-    dense, slots, weights = contribution(boundary_tiles, inverse_factor[0], coupling[0], tiles)
-    return solve(slots, weights, dense, bem_block[0, 0])[None, None]
+    return solve(boundary_tiles, inverse_factor[0], coupling[0], bem_block[0, 0])[None, None]
 
 
 def solution(mesh):

time: 123 us -> 118 us (0.959)
  the two profiles are of different devices: /device:TPU:1 before, /device:TPU:16 now
where the time goes in v3:
time: 118 us
  Pallas kernels  114 us (97%)
  local copies, waits for them, and re-layouts  3.78 us (3%)
    pallas_call x1, Pallas kernels, solve(): pl.pallas_call(solve_kernel, out_shape=jax.ShapeDtypeStruct(bem.shape, F3...  114 us
    unnamed x2, local copies, waits for them, and re-layouts  3.78 us

profile of v3, /device:TPU:16, one launch (start us, length us, event | category | flops | bytes accessed | tf_op | source)
XLA Modules:
  0.0 118.2 jit_solution(7288272271016222310)
XLA Ops:
  0.0 1.5 %copy.5.tiles_ref = s32[256,8]{1,0:T(8,128)} copy(s32[256,8]{0,1:T(8,128)} %param.6) | data formatting | bytes 16384 | tf_op args[2]
  1.5 114.4 %solve.1 = f32[128,2048]{1,0:T(8,128)} custom-call(s32[256,8]{1,0:T(8,128)} %copy.5.tiles_ref, bf16[1536,1536]{1,0:T(8,128)(2,1)} %bitcast.4, bf16[1536,1024]{1,0:T(8,128)(2,1)} %bitcast.6, f32[128,2048]{1,0:T(8,128)} %bitcast.7), custom_call_target="tpu_custom_call" | custom-call | tf_op jit(solution)/shard_map/solve/pallas_call | solution.py:658
  115.9 2.3 %copy.7 = f32[1,1,128,2048]{3,2,1,0:T(8,128)} copy(f32[1,1,128,2048]{3,2,1,0:T(8,128)} %bitcast.5) | data formatting | bytes 2097152

commit v4 on v3

--- a/solution.py
+++ b/solution.py
@@ -279,14 +279,6 @@
 
     lax.fori_loop(1, 16, place, 0)
     start(y_copies[0])
-    @pl.when(zh == 0)
-    def _():
-        @pl.when(y != 0)
-        def _():
-            arrive(ypart, py_recv)
-
-        start(pzs)
-
     b2 = copy(psum.at[1], pother, b2_send, b2_recv, partner)
     b3 = [
         copy(
@@ -323,14 +315,15 @@
         psum[0] = psum[0] + pother[...]
         start(b3)
 
+    @pl.when(zh == 0)
+    def _():
+        @pl.when(y != 0)
+        def _():
+            arrive(ypart, py_recv)
+
+        start(pzs)
+
     start(y_copies[1])
-    @pl.when(zh != 0)
-    def _():
-        arrive(ypart, pz_recv)
-
-    start(gy)
-    zpart[:, rows_of(y, 32)] = ypart[...]
-
 
     q0 = [copy(gq.at[mine], gq.at[mine], q0_send.at[d - 1], q0_recv, at_col(d)) for d in three]
     q1 = [
@@ -413,11 +406,15 @@
         one.wait_recv()
     start(q3)
     diag[:, rows_of(y, 32)] = g32[...]
+    @pl.when(zh != 0)
+    def _():
+        arrive(ypart, pz_recv)
+
+    start(gy)
+    zpart[:, rows_of(y, 32)] = ypart[...]
+
     start(y_copies[2])
-    for one in gy:
-        one.wait_recv()
-    start(gx)
-    panel[r] = zpart[...]
+    start(y_copies[3])
 
     swaps = [
         copy(
@@ -518,8 +515,6 @@
             def _():
                 cols[:, m * T : (m + 1) * T] = cols[:, m * T : (m + 1) * T] + turned
 
-    start(y_copies[3])
-
     identity = (
         lax.broadcasted_iota(jnp.int32, (T, T), 0) == lax.broadcasted_iota(jnp.int32, (T, T), 1)
     ).astype(F32)
@@ -528,6 +523,10 @@
     work[2 * T : 3 * T, :] = cols[:, 0:T]
     unit[...] = identity
     eliminate_part(work, unit, 0, 3 * T)
+    for one in gy:
+        one.wait_recv()
+    start(gx)
+    panel[r] = zpart[...]
     up, down = first_hop()
     eliminate_part(work, unit, 1, 3 * T)
     add_round(1)

time: 118 us -> 115 us (0.975)
  the two profiles are of different devices: /device:TPU:16 before, /device:TPU:1 now
where the time goes in v4:
time: 115 us; the launch traced here: 114 us
  Pallas kernels  110 us (96%)
  local copies, waits for them, and re-layouts  3.78 us (3%)
    pallas_call x1, Pallas kernels, solve(): pl.pallas_call(solve_kernel, out_shape=jax.ShapeDtypeStruct(bem.shape, F3...  110 us
    unnamed x2, local copies, waits for them, and re-layouts  3.78 us

profile of v4, /device:TPU:1, one launch (start us, length us, event | category | flops | bytes accessed | tf_op | source)
XLA Modules:
  0.0 114.1 jit_solution(13830489363521875758)
XLA Ops:
  0.0 1.5 %copy.5.tiles_ref = s32[256,8]{1,0:T(8,128)} copy(s32[256,8]{0,1:T(8,128)} %param.6) | data formatting | bytes 16384 | tf_op args[2]
  1.5 110.3 %solve.1 = f32[128,2048]{1,0:T(8,128)} custom-call(s32[256,8]{1,0:T(8,128)} %copy.5.tiles_ref, bf16[1536,1536]{1,0:T(8,128)(2,1)} %bitcast.4, bf16[1536,1024]{1,0:T(8,128)(2,1)} %bitcast.6, f32[128,2048]{1,0:T(8,128)} %bitcast.7), custom_call_target="tpu_custom_call" | custom-call | tf_op jit(solution)/shard_map/solve/pallas_call | solution.py:657
  111.8 2.3 %copy.7 = f32[1,1,128,2048]{3,2,1,0:T(8,128)} copy(f32[1,1,128,2048]{3,2,1,0:T(8,128)} %bitcast.5) | data formatting | bytes 2097152
